TPU v7x, 256 devices: a whole 4x4x8 slice. The times are simulated.
256 devices in a mesh: row: 8 (over y, core), col: 32 (over x, z).
Axes of the slice: x: 4, y: 4, z: 8, core: 2. Of those that a mesh axis runs over, the one named last changes fastest.
Arguments:
- matrix: bfloat16 [24576, 24576], P('row', 'col'), may hold values from -8 to 8
- panels: float32 [2, 24576, 128], P(None, ('col', 'row')), may hold values from -0.0390625 to 0.0390625
Outputs:
- updated: bfloat16 [24576, 24576], P('row', 'col')
All inputs are finite; a program needn't handle non-finite values.
Results may differ from a plain program's by a relative error of at most 0.0038.
The roundings to bfloat16 on the way count: a program that leaves them out, or rounds other values in their place, can miss the bound.
Values may be sent and summed in bfloat16 or wider, within the bound.
A program may use at most 64 MiB of HBM per device.

v0:
```python
import jax
import jax.numpy as jnp
from jax import lax
from jax.sharding import PartitionSpec as P


def reflector(gram):
    lower = jnp.linalg.cholesky(gram)
    return jax.scipy.linalg.cho_solve((lower, True), 2.0 * jnp.eye(gram.shape[0], dtype=gram.dtype))


def exact_dot(left, right):
    return jnp.dot(left, right, precision=lax.Precision.HIGHEST)


def column_block(piece):
    return lax.all_gather(piece, "row", axis=0, tiled=True)


def row_block(col_piece):
    n_row = lax.axis_size("row")
    n_col = lax.axis_size("col")
    everything = lax.all_gather(col_piece, "col", axis=0, tiled=True)
    height = col_piece.shape[0] * (n_col // n_row)
    return lax.dynamic_slice_in_dim(everything, lax.axis_index("row") * height, height, 0)


def apply_panel(local, vectors, factor):
    vb = vectors.astype(jnp.bfloat16)
    col_v = column_block(vb)
    row_v = row_block(col_v)
    product = lax.psum_scatter(
        lax.dot_general(local, row_v, (((0,), (0,)), ((), ())), preferred_element_type=jnp.float32),
        "row",
        scatter_dimension=0,
        tiled=True,
    )
    scaled = exact_dot(product, factor)
    coupling = lax.psum(exact_dot(vectors.T, scaled), ("row", "col"))
    wide = scaled - 0.5 * exact_dot(vectors, exact_dot(factor, coupling))
    wb = wide.astype(jnp.bfloat16)
    col_w = column_block(wb)
    row_w = row_block(col_w)
    left = jnp.concatenate([row_v, row_w], axis=1)
    right = jnp.concatenate([col_w, col_v], axis=1)
    update = lax.dot_general(
        left, right, (((1,), (1,)), ((), ())), preferred_element_type=jnp.float32
    )
    return (local.astype(jnp.float32) - update).astype(jnp.bfloat16)


def per_device(matrix, panels):
    first = panels[0]
    raw_second = panels[1]
    gram_one, cross = lax.psum(
        (exact_dot(first.T, first), exact_dot(first.T, raw_second)), ("row", "col")
    )
    factor_one = reflector(gram_one)
    mixing = exact_dot(factor_one, cross)
    second = raw_second - exact_dot(first, mixing)
    gram_two = lax.psum(exact_dot(second.T, second), ("row", "col"))
    factor_two = reflector(gram_two)
    current = apply_panel(matrix, first, factor_one)
    current = apply_panel(current, second, factor_two)
    return current


def solution(mesh):
    placed = (P("row", "col"), P(None, ("col", "row"), None))
    return jax.shard_map(
        per_device, mesh=mesh, in_specs=placed, out_specs=P("row", "col"), check_vma=False
    )
```

profile of v0, /device:TPU:1, one launch (start us, length us, event | category | flops | bytes accessed | tf_op | source)
XLA Modules:
  0.0 1077.5 jit_solution(13611042611158275653)
XLA Ops:
  7.4 1.8 fusion.38
  9.2 1.7 fusion.32
  11.8 16.9 %all_gather.24 = bf16[768,128]{1,0:T(8,128)(2,1)} all-gather(bf16[96,128]{1,0:T(8,128)(2,1)S(1)} %bitcast_convert_fusion), channel_id=1, replica_groups=mesh['row'=8,'col'=32] {'row'}, dimensions={0}, use_global_device_ids=true | all-gather | bytes 221184 | tf_op jit(solution)/shard_map/all_gather | solution.py:17
  28.8 240.5 %all-reduce.10.cloned.1.call-done = (f32[128,128]{0,1:T(8,128)}, f32[128,128]{1,0:T(8,128)}) async-done(((f32[128,128]{0,1:T(8,128)}, f32[128,128]{1,0:T(8,128)}), (f32[128,128]{0,1:T(8,128)}, f32[128,128]{1,0:T(8,128)})) %all-reduce.10.cloned.1.call-update) | async-done | bytes 131088 | tf_op jit(solution)/shard_map/psum | solution.py:55
  271.1 11.7 %cholesky.44 = f32[128,128]{1,0:T(8,128)S(1)} custom-call(f32[128,128]{1,0:T(8,128)S(1)} %fusion.31), custom_call_target="Cholesky" | custom-call | tf_op jit(solution)/shard_map/jit(cholesky)/cholesky | solution.py:8
  284.2 9.8 custom-call.8
  294.3 1.2 constant_dynamic-slice_fusion.3
  295.5 3.2 convolution_bitcast_fusion
  301.3 27.2 %reduce-scatter.7.cloned.1.call-done = f32[96,128]{1,0:T(8,128)} async-done(((f32[768,128]{1,0:T(8,128)}), f32[96,128]{1,0:T(8,128)}) %reduce-scatter.7.cloned.1.call-update) | async-done | bytes 49168
  330.5 16.7 %all_gather.28 = bf16[768,128]{1,0:T(8,128)(2,1)} all-gather(bf16[96,128]{1,0:T(8,128)(2,1)S(1)} %get-tuple-element.11), channel_id=1, replica_groups=mesh['row'=8,'col'=32] {'row'}, dimensions={0}, use_global_device_ids=true | all-gather | bytes 221184 | tf_op jit(solution)/shard_map/all_gather | solution.py:17
  347.2 236.6 %all-reduce.8.cloned.1.call-done = (f32[128,128]{0,1:T(8,128)}, f32[128,128]{0,1:T(8,128)}) async-done(((f32[128,128]{0,1:T(8,128)}, f32[128,128]{0,1:T(8,128)}), (f32[128,128]{0,1:T(8,128)}, f32[128,128]{0,1:T(8,128)})) %all-reduce.8.cloned.1.call-update) | async-done | bytes 131088 | tf_op jit(solution)/shard_map/psum | solution.py:39
  585.1 15.7 %all_gather.26 = bf16[768,128]{1,0:T(8,128)(2,1)} all-gather(bf16[96,128]{1,0:T(8,128)(2,1)S(1)} %fusion.10), channel_id=1, replica_groups=mesh['row'=8,'col'=32] {'row'}, dimensions={0}, use_global_device_ids=true | all-gather | bytes 221184 | tf_op jit(solution)/shard_map/all_gather | solution.py:17
  601.1 1.2 constant_dynamic-slice_fusion.1
  604.1 11.7 %cholesky.55 = f32[128,128]{1,0:T(8,128)S(1)} custom-call(f32[128,128]{1,0:T(8,128)S(1)} %fusion.27), custom_call_target="Cholesky" | custom-call | tf_op jit(solution)/shard_map/jit(cholesky)/cholesky | solution.py:8
  615.8 68.8 %all-gather.7.cloned.1.call-done = bf16[24576,128]{1,0:T(8,128)(2,1)} async-done(((bf16[768,128]{1,0:T(8,128)(2,1)}), bf16[24576,128]{1,0:T(8,128)(2,1)}) %all-gather.7.cloned.1.call-update) | async-done | bytes 6291472 | tf_op jit(solution)/shard_map/all_gather | solution.py:23
  685.8 3.9 subtract_convert_fusion.1
  689.7 2.2 copy-done
  691.9 2.2 fusion.60
  695.5 9.8 custom-call.9
  705.8 16.9 %reduce-scatter.5.cloned.1.call-done = f32[96,128]{1,0:T(8,128)} async-done(((f32[768,128]{1,0:T(8,128)}), f32[96,128]{1,0:T(8,128)}) %reduce-scatter.5.cloned.1.call-update) | async-done | bytes 49168 | tf_op jit(solution)/shard_map/reduce_scatter | solution.py:32
  724.8 239.4 %all-reduce.6.cloned.1.call-done = f32[128,128]{1,0:T(8,128)} async-done(((f32[128,128]{1,0:T(8,128)}), f32[128,128]{1,0:T(8,128)}) %all-reduce.6.cloned.1.call-update) | async-done | bytes 65552 | tf_op jit(solution)/shard_map/psum | solution.py:39
  965.4 13.5 %all_gather.30 = bf16[768,128]{1,0:T(8,128)(2,1)} all-gather(bf16[96,128]{1,0:T(8,128)(2,1)S(1)} %fusion.11), channel_id=1, replica_groups=mesh['row'=8,'col'=32] {'row'}, dimensions={0}, use_global_device_ids=true | all-gather | bytes 221184 | tf_op jit(solution)/shard_map/all_gather | solution.py:17
  979.0 84.2 %all-gather.11.cloned.1.call-done = bf16[24576,128]{1,0:T(8,128)(2,1)} async-done(((bf16[768,128]{1,0:T(8,128)(2,1)}), bf16[24576,128]{1,0:T(8,128)(2,1)}) %all-gather.11.cloned.1.call-update) | async-done | bytes 6291472 | tf_op jit(solution)/shard_map/all_gather | solution.py:23
  1064.3 6.1 subtract_convert_fusion
  (58 shorter events, 19.9 us)
Async XLA Ops:
  7.4 261.9 %all-reduce.10.cloned.1.call-start = ((), (), s32[]{:S(2)}) async-start(), calls=%async_computation.10 | async-start | bytes 262144 | tf_op jit(solution)/shard_map/psum | solution.py:55
  10.9 283.4 %all-gather.5.cloned.1.call-start = ((), (), s32[]{:S(2)}) async-start(), calls=%async_computation.2 | async-start | bytes 6488064 | tf_op jit(solution)/shard_map/all_gather | solution.py:23
  28.7 299.8 %reduce-scatter.7.cloned.1.call-start = ((), (), s32[]{:S(2)}) async-start(), calls=%async_computation.8 | async-start | bytes 442368
  270.2 29.7 %copy-start.4 = (f32[128,128]{1,0:T(8,128)S(1)}, f32[128,128]{1,0:T(8,128)}, u32[]{:S(2)}) copy-start(f32[128,128]{1,0:T(8,128)} %get-tuple-element.10) | copy-start | bytes 196612
  271.1 29.0 %copy-start.1 = (f32[2,96,128]{2,1,0:T(8,128)S(1)}, f32[2,96,128]{2,1,0:T(8,128)}, u32[]{:S(2)}) copy-start(f32[2,96,128]{2,1,0:T(8,128)} %param.6) | copy-start | bytes 294916
  298.7 387.1 %copy-start.2 = (bf16[768,128]{1,0:T(8,128)(2,1)S(1)}, bf16[768,128]{1,0:T(8,128)(2,1)}, u32[]{:S(2)}) copy-start(bf16[768,128]{1,0:T(8,128)(2,1)} %all_gather.24) | copy-start | bytes 589828
  299.7 284.2 %all-reduce.8.cloned.1.call-start = ((), (), s32[]{:S(2)}) async-start(), calls=%async_computation.9 | async-start | bytes 262144 | tf_op jit(solution)/shard_map/psum | solution.py:39
  330.4 270.7 %all-gather.9.cloned.1.call-start = ((), (), s32[]{:S(2)}) async-start(), calls=%async_computation.4 | async-start | bytes 6488064 | tf_op jit(solution)/shard_map/all_gather | solution.py:23
  347.2 337.4 %all-gather.7.cloned.1.call-start = ((), (), s32[]{:S(2)}) async-start(), calls=%async_computation.3 | async-start | bytes 6488064 | tf_op jit(solution)/shard_map/all_gather | solution.py:23
  600.8 122.0 %reduce-scatter.5.cloned.1.call-start = ((), (), s32[]{:S(2)}) async-start(), calls=%async_computation.5 | async-start | bytes 442368 | tf_op jit(solution)/shard_map/reduce_scatter | solution.py:32
  689.7 2.2 copy-start
  691.9 372.5 %copy-start.3 = (bf16[768,128]{1,0:T(8,128)(2,1)S(1)}, bf16[768,128]{1,0:T(8,128)(2,1)}, u32[]{:S(2)}) copy-start(bf16[768,128]{1,0:T(8,128)(2,1)} %all_gather.28) | copy-start | bytes 589828
  694.1 270.1 %all-reduce.6.cloned.1.call-start = ((), (), s32[]{:S(2)}) async-start(), calls=%async_computation.6 | async-start | bytes 131072 | tf_op jit(solution)/shard_map/psum | solution.py:39
  724.7 338.4 %all-gather.11.cloned.1.call-start = ((), (), s32[]{:S(2)}) async-start(), calls=%async_computation.7 | async-start | bytes 6488064 | tf_op jit(solution)/shard_map/all_gather | solution.py:23
Sparse Core Ops, SparseCore 0:
  14.7 254.5 all-reduce.9
  330.5 253.2 all-reduce.7
  724.8 239.2 all-reduce.5
Sparse Core Ops, SparseCore 1:
  28.8 88.6 all-gather.4
  299.7 28.7 reduce-scatter.6
  347.2 87.3 all-gather.8
  600.9 83.6 all-gather.6
  694.2 28.6 reduce-scatter.4
  979.1 84.0 all-gather.10
where the time goes:
time: 1080 us
  waiting for transfers between devices  914 us (85%)
  blocking collectives  62.7 us (6%)
  other arithmetic  47.5 us (4%)
  matrix products  27.5 us (3%)
  between operations  14.9 us (1%)
    psum x2, waiting for transfers between devices, apply_panel(): coupling = lax.psum(exact_dot(vectors.T, scaled), ('row', 'col'))  476 us
    psum x1, waiting for transfers between devices, per_device(): lax.psum((exact_dot(first.T, first), exact_dot(first.T, raw_second)), ('r...  241 us
    all_gather x4, waiting for transfers between devices, row_block(): everything = lax.all_gather(col_piece, 'col', axis=0, tiled=True)  153 us
    all_gather x4, blocking collectives, column_block(): return lax.all_gather(piece, 'row', axis=0, tiled=True)  62.7 us
    unnamed x10, waiting for transfers between devices  27.3 us
    another operation x6, other arithmetic, reflector(): lower = jnp.linalg.cholesky(gram)  24.8 us
  transfers between devices with their start and end apart: 9, of which 7 were waited for; matrix products, arithmetic and copies ran while one was open for 5% of the time, Pallas kernels for 0%

commit v1 on v0

v1 whole, which is shorter than its diff:
```python
import functools

import jax
import jax.numpy as jnp
from jax import lax
from jax.experimental import pallas as pl
from jax.experimental.pallas import tpu as pltpu
from jax.sharding import PartitionSpec as P

NB = 128
PIECE = 96
BLOCK = 768
ROWS = 3072
F32 = jnp.float32
BF16 = jnp.bfloat16


def fdot(left, right, contract=((1,), (0,))):
    return lax.dot_general(
        left, right, (contract, ((), ())), precision=lax.Precision.HIGHEST, preferred_element_type=F32
    )


def rcopy(src, dst, send, recv, row, col):
    return pltpu.make_async_remote_copy(
        src_ref=src, dst_ref=dst, send_sem=send, recv_sem=recv,
        device_id=(row, col), device_id_type=pl.DeviceIdType.MESH,
    )


class Where:
    def __init__(self):
        self.r = lax.axis_index("row")
        self.c = lax.axis_index("col")
        self.y = self.r // 2
        self.k = self.r % 2
        self.x = self.c // 8
        self.z = self.c % 8


def loop(lo, hi, body):
    def step(i, carry):
        body(i)
        return carry
    lax.fori_loop(lo, hi, step, 0)


class AllReduce:
    def __init__(self, w, src, refs):
        self.w = w
        self.src = src
        (self.in1, self.acc, self.in2, self.in3, self.g4, self.out,
         self.s1, self.q1, self.s2, self.q2, self.s3, self.q3, self.s4, self.q4, self.s5, self.q5) = refs

    def copy1(self, d):
        w = self.w
        to = (w.r + d) % 8
        return rcopy(self.src.at[pl.ds(pl.multiple_of(to * 64, 64), 64)], self.in1.at[d - 1],
                     self.s1.at[d - 1], self.q1.at[d - 1], to, w.c)

    def copy2(self, d):
        w = self.w
        to = (w.z + d) % 8
        return rcopy(self.acc.at[pl.ds(pl.multiple_of(to * 8, 8), 8)], self.in2.at[d - 1],
                     self.s2.at[d - 1], self.q2.at[d - 1], w.r, w.x * 8 + to)

    def copy3(self, d):
        w = self.w
        to = (w.x + d) % 4
        return rcopy(self.in3.at[0], self.in3.at[d], self.s3.at[d - 1], self.q3.at[d - 1], w.r, to * 8 + w.z)

    def copy4(self, d, owner):
        w = self.w
        to = (w.z + d) % 8
        part = self.g4.at[pl.ds(pl.multiple_of(owner * 8, 8), 8)]
        return rcopy(part, part, self.s4.at[d - 1], self.q4.at[d - 1], w.r, w.x * 8 + to)

    def copy5(self, d, owner):
        w = self.w
        to = (w.r + d) % 8
        part = self.out.at[pl.ds(pl.multiple_of(owner * 64, 64), 64)]
        return rcopy(part, part, self.s5.at[d - 1], self.q5.at[d - 1], to, w.c)

    def step1(self):
        loop(1, 8, lambda d: self.copy1(d).start())

    def step2(self):
        loop(1, 8, lambda d: self.copy1(d).wait_recv())
        total = self.src[pl.ds(pl.multiple_of(self.w.r * 64, 64), 64)]
        for d in range(7):
            total = total + self.in1[d]
        self.acc[...] = total
        loop(1, 8, lambda d: self.copy2(d).start())

    def step3(self):
        loop(1, 8, lambda d: self.copy2(d).wait_recv())
        total = self.acc[pl.ds(pl.multiple_of(self.w.z * 8, 8), 8)]
        for d in range(7):
            total = total + self.in2[d]
        self.in3[0] = total
        loop(1, 4, lambda d: self.copy3(d).start())

    def step4(self):
        z = self.w.z
        loop(1, 4, lambda d: self.copy3(d).wait_recv())
        total = (self.in3[0] + self.in3[2]) + (self.in3[1] + self.in3[3])
        self.g4[pl.ds(pl.multiple_of(z * 8, 8), 8)] = total
        loop(1, 8, lambda d: self.copy4(d, z).start())

    def step5(self):
        w = self.w
        loop(1, 8, lambda d: self.copy4(d, (w.z - d + 8) % 8).wait_recv())
        self.out[pl.ds(pl.multiple_of(w.r * 64, 64), 64)] = self.g4[...]
        loop(1, 8, lambda d: self.copy5(d, w.r).start())

    def finish(self):
        w = self.w
        loop(1, 8, lambda d: self.copy5(d, (w.r - d + 8) % 8).wait_recv())

    def drain(self):
        w = self.w
        loop(1, 8, lambda d: self.copy1(d).wait_send())
        loop(1, 8, lambda d: self.copy2(d).wait_send())
        loop(1, 4, lambda d: self.copy3(d).wait_send())
        loop(1, 8, lambda d: self.copy4(d, w.z).wait_send())
        loop(1, 8, lambda d: self.copy5(d, w.r).wait_send())


class Gather:
    def __init__(self, w, piece, rows, cols, sems):
        self.w = w
        self.piece = piece
        self.rows = rows
        self.cols = cols
        self.cs, self.cq, self.xs, self.xq, self.zs, self.zq = sems

    def col_copy(self, d, owner):
        w = self.w
        return rcopy(self.piece, self.cols.at[pl.ds(pl.multiple_of(owner * PIECE, PIECE), PIECE)],
                     self.cs.at[d - 1], self.cq.at[d - 1], (w.r + d) % 8, w.c)

    def x_copy(self, d, owner):
        w = self.w
        at = pl.multiple_of((w.z % 4) * BLOCK + owner * PIECE, PIECE)
        return rcopy(self.piece, self.rows.at[pl.ds(at, PIECE)], self.xs.at[d], self.xq.at[owner],
                     2 * w.x + w.z // 4, ((w.x + d) % 4) * 8 + w.z)

    def z_copy(self, way, t, at_z):
        w = self.w
        src_z = (at_z - t + 8) % 8 if way == 0 else (at_z + t) % 8
        base = (src_z % 4) * BLOCK
        if t < 3:
            part = self.rows.at[pl.ds(pl.multiple_of(base, BLOCK), BLOCK)]
        else:
            half = BLOCK // 2
            part = self.rows.at[pl.ds(pl.multiple_of(base + way * half, half), half)]
        to = (w.z + 1) % 8 if way == 0 else (w.z + 7) % 8
        copy = rcopy(part, part, self.zs.at[way, t], self.zq.at[way, t], w.r, w.x * 8 + to)
        return copy, src_z // 4 == w.k

    def start(self):
        w = self.w
        for d in range(1, 4):
            self.x_copy(d, w.r).start()
        self_target = w.r == 2 * w.x + w.z // 4

        @pl.when(jnp.logical_not(self_target))
        def _():
            self.x_copy(0, w.r).start()

        @pl.when(self_target)
        def _():
            at = pl.multiple_of((w.z % 4) * BLOCK + w.r * PIECE, PIECE)
            self.rows[pl.ds(at, PIECE)] = self.piece[...]

        loop(1, 8, lambda d: self.col_copy(d, w.r).start())
        self.cols[pl.ds(pl.multiple_of(w.r * PIECE, PIECE), PIECE)] = self.piece[...]

    def wait_x(self):
        w = self.w

        @pl.when(w.z // 4 == w.k)
        def _():
            def one(owner):
                @pl.when(jnp.logical_not(jnp.logical_and(owner == w.r, w.x == w.y)))
                def _():
                    self.x_copy(0, owner).wait_recv()
            loop(0, 8, one)

    def send_z(self, t):
        for way in range(2):
            copy, mine = self.z_copy(way, t, self.w.z)

            @pl.when(mine)
            def _():
                copy.start()

    def wait_z(self, t):
        z = self.w.z
        for way in range(2):
            copy, mine = self.z_copy(way, t, (z + 7) % 8 if way == 0 else (z + 1) % 8)

            @pl.when(mine)
            def _():
                copy.wait_recv()

    def step(self, t):
        if t == 0:
            self.wait_x()
        else:
            self.wait_z(t - 1)
        if t < 4:
            self.send_z(t)

    def wait_cols(self):
        w = self.w
        loop(1, 8, lambda d: self.col_copy(d, (w.r - d + 8) % 8).wait_recv())

    def drain(self):
        w = self.w
        for d in range(1, 4):
            self.x_copy(d, w.r).wait_send()

        @pl.when(w.r != 2 * w.x + w.z // 4)
        def _():
            self.x_copy(0, w.r).wait_send()

        loop(1, 8, lambda d: self.col_copy(d, w.r).wait_send())
        for t in range(4):
            for way in range(2):
                copy, mine = self.z_copy(way, t, w.z)

                @pl.when(mine)
                def _():
                    copy.wait_send()


def invert(work, lo, hi):
    sub = lax.broadcasted_iota(jnp.int32, (8, 2 * NB), 0)

    def panel(p):
        at = pl.multiple_of(p * 8, 8)
        for m in range(2):
            rows = work[m, pl.ds(at, 8), :]
            for j in range(8):
                pivot = rows[j:j + 1, :] / rows[j:j + 1, j:j + 1]
                rows = jnp.where(sub == j, pivot, rows - rows[:, j:j + 1] * pivot)
            whole = work[m]
            new = whole
            for j in range(8):
                new = new - whole[:, j:j + 1] * rows[j:j + 1, :]
            work[m, :, 0:NB] = pltpu.roll(new[:, :NB], NB - 8, 1)
            work[m, :, NB:] = new[:, NB:]
            work[m, pl.ds(at, 8), 0:NB] = pltpu.roll(rows[:, :NB], NB - 8, 1)
            work[m, pl.ds(at, 8), NB:] = rows[:, NB:]
    loop(lo, hi, panel)


def kernel(a_hbm, pan, out, a, piece_x, piece_v, piece_w, rows_x, rows_v, rows_w, cols_x, cols_v, cols_w,
           gram, inner, yt, y, y_in, work, load_sem, store_sem, ys, yq, *rest):
    w = Where()
    n_ar = 16
    ar_g = AllReduce(w, gram, rest[:n_ar])
    ar_s = AllReduce(w, inner, rest[n_ar:2 * n_ar])
    sems = rest[2 * n_ar:]
    g_x = Gather(w, piece_x, rows_x, cols_x, sems[0:6])
    g_v = Gather(w, piece_v, rows_v, cols_v, sems[6:12])
    g_w = Gather(w, piece_w, rows_w, cols_w, sems[12:18])

    load = pltpu.make_async_copy(a_hbm, a, load_sem)
    load.start()
    v1 = pan[0]
    p2 = pan[1]
    piece_x[:, 0:NB] = v1.astype(BF16)
    piece_x[:, NB:] = p2.astype(BF16)
    g_x.start()
    both = jnp.concatenate([v1, p2], axis=1)
    gram[0:256] = fdot(both, v1, ((0,), (0,)))
    gram[256:512] = fdot(both, p2, ((0,), (0,)))
    ar_g.step1()
    g_x.step(0)
    ar_g.step2()
    g_x.step(1)
    ar_g.step3()
    g_x.step(2)
    ar_g.step4()
    g_x.step(3)
    ar_g.step5()
    g_x.step(4)
    load.wait()

    yt[...] = jnp.zeros_like(yt)

    def product(i):
        at = pl.ds(pl.multiple_of(i * 256, 256), 256)
        yt[...] += lax.dot_general(rows_x[at], a[at], (((0,), (0,)), ((), ())), preferred_element_type=F32)
    loop(0, ROWS // 256, product)
    y[...] = yt[...].T
    g_x.wait_cols()

    def y_copy(d):
        to = (w.r + d) % 8
        return rcopy(y.at[pl.ds(pl.multiple_of(to * PIECE, PIECE), PIECE)], y_in.at[d - 1],
                     ys.at[d - 1], yq.at[d - 1], to, w.c)

    hi = yt[...].astype(BF16)
    lo = (yt[...] - hi.astype(F32)).astype(BF16)
    s_t = (lax.dot_general(hi, cols_x[...], (((1,), (0,)), ((), ())), preferred_element_type=F32)
           + lax.dot_general(lo, cols_x[...], (((1,), (0,)), ((), ())), preferred_element_type=F32))
    inner[0:256] = s_t[:, 0:NB]
    inner[256:512] = s_t[:, NB:]
    ar_s.step1()
    loop(1, 8, lambda d: y_copy(d).start())

    ar_g.finish()
    g1 = ar_g.out[0:128]
    cross = ar_g.out[256:384]
    g2 = ar_g.out[384:512]
    eye2 = jnp.where(lax.broadcasted_iota(jnp.int32, (NB, NB), 0) == lax.broadcasted_iota(jnp.int32, (NB, NB), 1),
                     2.0, 0.0).astype(F32)
    work[0, :, 0:NB] = g1
    work[1, :, 0:NB] = g2
    work[0, :, NB:] = eye2
    work[1, :, NB:] = eye2
    invert(work, 0, 4)
    ar_s.step2()
    invert(work, 4, 8)
    ar_s.step3()
    invert(work, 8, 12)
    ar_s.step4()
    invert(work, 12, 16)
    ar_s.step5()
    f1 = work[0, :, NB:]
    f2 = work[1, :, NB:]
    mix = fdot(f1, cross)
    v2 = p2 - fdot(v1, mix)
    piece_v[...] = v2.astype(BF16)
    g_v.start()

    loop(1, 8, lambda d: y_copy(d).wait_recv())
    total = y[pl.ds(pl.multiple_of(w.r * PIECE, PIECE), PIECE)]
    for d in range(7):
        total = total + y_in[d]
    y1 = total[:, 0:NB]
    y2 = total[:, NB:] - fdot(y1, mix)
    ar_s.finish()
    g_v.step(0)
    s11 = ar_s.out[0:128]
    s21 = ar_s.out[128:256]
    s12 = ar_s.out[256:384]
    s22 = ar_s.out[384:512]
    tt = (((0,), (0,)))
    b12 = s12 - fdot(s11, mix)
    b21 = s21 - fdot(mix, s11, tt)
    b22 = s22 - fdot(s21, mix) - fdot(mix, b12, tt)
    k1 = fdot(s11, f1, tt)
    l1 = 0.5 * fdot(f1, k1)
    g_v.step(1)
    h = fdot(f1, b12, tt) + fdot(l1, cross, tt)
    hc = fdot(h, cross, tt)
    k2 = fdot(b22.T + hc + hc.T, f2)
    l2 = 0.5 * fdot(f2, k2)
    w1 = fdot(y1, f1) - fdot(v1, l1)
    prod2 = y2 + fdot(w1, cross) - fdot(v1, h)
    w2 = fdot(prod2, f2) - fdot(v2, l2)
    piece_w[:, 0:NB] = w1.astype(BF16)
    piece_w[:, NB:] = w2.astype(BF16)
    g_w.start()
    g_v.step(2)
    g_w.step(0)
    g_v.step(3)
    g_w.step(1)
    g_v.step(4)
    g_w.step(2)
    g_w.step(3)
    g_w.step(4)
    g_v.wait_cols()
    g_w.wait_cols()

    def store(i):
        at = pl.ds(pl.multiple_of(i * 256, 256), 256)
        return pltpu.make_async_copy(a.at[at], out.at[at], store_sem.at[i])

    right1 = jnp.concatenate([cols_w[:, 0:NB], cols_x[:, 0:NB]], axis=1)
    right2 = jnp.concatenate([cols_w[:, NB:], cols_v[...]], axis=1)

    def update(i):
        at = pl.ds(pl.multiple_of(i * 256, 256), 256)
        nt = (((1,), (1,)), ((), ()))
        left1 = jnp.concatenate([rows_x[at, 0:NB], rows_w[at, 0:NB]], axis=1)
        left2 = jnp.concatenate([rows_v[at, :], rows_w[at, NB:]], axis=1)
        one = (a[at].astype(F32) - lax.dot_general(left1, right1, nt, preferred_element_type=F32)).astype(BF16)
        two = one.astype(F32) - lax.dot_general(left2, right2, nt, preferred_element_type=F32)
        a[at] = two.astype(BF16)
        store(i).start()
    loop(0, ROWS // 256, update)

    ar_g.drain()
    ar_s.drain()
    g_x.drain()
    g_v.drain()
    g_w.drain()
    loop(1, 8, lambda d: y_copy(d).wait_send())
    loop(0, ROWS // 256, lambda i: store(i).wait())


def scratch():
    vm = pltpu.VMEM
    dma = pltpu.SemaphoreType.DMA
    shapes = [
        vm((ROWS, BLOCK), BF16),
        vm((PIECE, 256), BF16), vm((PIECE, 128), BF16), vm((PIECE, 256), BF16),
        vm((ROWS, 256), BF16), vm((ROWS, 128), BF16), vm((ROWS, 256), BF16),
        vm((BLOCK, 256), BF16), vm((BLOCK, 128), BF16), vm((BLOCK, 256), BF16),
        vm((512, 128), F32), vm((512, 128), F32),
        vm((256, BLOCK), F32), vm((BLOCK, 256), F32), vm((7, PIECE, 256), F32),
        vm((2, NB, 2 * NB), F32),
        dma(()), dma((ROWS // 256,)), dma((7,)), dma((7,)),
    ]
    for _ in range(2):
        shapes += [
            vm((7, 64, 128), F32), vm((64, 128), F32), vm((7, 8, 128), F32), vm((4, 8, 128), F32),
            vm((64, 128), F32), vm((512, 128), F32),
            dma((7,)), dma((7,)), dma((7,)), dma((7,)), dma((3,)), dma((3,)), dma((7,)), dma((7,)), dma((7,)), dma((7,)),
        ]
    for _ in range(3):
        shapes += [dma((7,)), dma((7,)), dma((4,)), dma((8,)), dma((2, 4)), dma((2, 4))]
    return shapes


def per_device(matrix, panels):
    return pl.pallas_call(
        kernel,
        out_shape=jax.ShapeDtypeStruct((ROWS, BLOCK), BF16),
        in_specs=[pl.BlockSpec(memory_space=pl.ANY), pl.BlockSpec(memory_space=pltpu.VMEM)],
        out_specs=pl.BlockSpec(memory_space=pl.ANY),
        scratch_shapes=scratch(),
        compiler_params=pltpu.CompilerParams(has_side_effects=True, vmem_limit_bytes=48 * 1024 * 1024),
        cost_estimate=pl.CostEstimate(flops=3700000000, bytes_accessed=9437184, transcendentals=0),
    )(matrix, panels)


def solution(mesh):
    placed = (P("row", "col"), P(None, ("col", "row"), None))
    return jax.shard_map(
        per_device, mesh=mesh, in_specs=placed, out_specs=P("row", "col"), check_vma=False
    )
```

time: 1080 us -> 135 us (0.12)
  waiting for transfers between devices: 914 us -> 0 us
  Pallas kernels: 0 us -> 132 us
  blocking collectives: 62.7 us -> 0 us
  other arithmetic: 47.5 us -> 0 us
  matrix products: 27.5 us -> 0 us
  between operations: 14.9 us -> 0.01 us
    psum x3 -> x0, waiting for transfers between devices: 717 us -> none  [the longest x2 476 us: apply_panel(): coupling = lax.psum(exact_dot(vectors.T, scaled), ('row', 'col'))]
    all_gather x4 -> x0, waiting for transfers between devices: 153 us -> none  [row_block(): everything = lax.all_gather(col_piece, 'col', axis=0, tiled=True)]
    pallas_call x0 -> x1, Pallas kernels: none -> 132 us  [per_device(): pl.pallas_call(kernel, out_shape=jax.ShapeDtypeStruct((ROWS, BLOCK), BF16...]
    all_gather x4 -> x0, blocking collectives: 62.7 us -> none  [column_block(): return lax.all_gather(piece, 'row', axis=0, tiled=True)]
    another operation x10 -> x0, other arithmetic: 45.8 us -> none  [the longest x6 24.8 us: reflector(): lower = jnp.linalg.cholesky(gram)]
    unnamed x10 -> x0, waiting for transfers between devices: 27.3 us -> none
    dot_general x17 -> x0, matrix products: 26.5 us -> none  [the longest x13 11.2 us: exact_dot(): return jnp.dot(left, right, precision=lax.Precision.HIGHEST)]
    reduce_scatter x1 -> x0, waiting for transfers between devices: 16.9 us -> none  [apply_panel(): lax.psum_scatter(lax.dot_general(local, row_v, (((0,), (0,)), ((), ())),...]
  transfers between devices with their start and end apart: 9 -> 0, of which waited for: 7 -> 0; matrix products, arithmetic and copies ran while one was open for 5% -> 0% of each run, Pallas kernels for 0% -> 0%
where the time goes in v1:
time: 135 us
  Pallas kernels  132 us (98%)
  local copies, waits for them, and re-layouts  3.08 us (2%)
    pallas_call x1, Pallas kernels, per_device(): pl.pallas_call(kernel, out_shape=jax.ShapeDtypeStruct((ROWS, BLOCK), BF16...  132 us
    unnamed x3, local copies, waits for them, and re-layouts  3.08 us

profile of v1, /device:TPU:1, one launch (start us, length us, event | category | flops | bytes accessed | tf_op | source)
XLA Modules:
  0.0 135.4 jit_solution(3900529874157109572)
XLA Ops:
  0.0 0.0 copy-start
  0.0 0.9 copy-done
  0.9 132.3 %shard_map.28 = bf16[3072,768]{1,0:T(8,128)(2,1)S(1)} custom-call(bf16[3072,768]{1,0:T(8,128)(2,1)} %a_hbm.1, f32[2,96,128]{2,1,0:T(8,128)S(1)} %copy-done), custom_call_target="tpu_custom_call" | custom-call | flops 3700000000 | bytes 9437184 | tf_op jit(solution)/shard_map/pallas_call | solution.py:432
  133.2 2.2 %copy.4 = bf16[3072,768]{1,0:T(8,128)(2,1)} copy(bf16[3072,768]{1,0:T(8,128)(2,1)S(1)} %shard_map.28) | data formatting | bytes 9437184
Async XLA Ops:
  0.0 0.9 copy-start

commit v2 on v1

--- a/solution.py
+++ b/solution.py
@@ -256,16 +256,55 @@
     loop(lo, hi, panel)
 
 
-def kernel(a_hbm, pan, out, a, piece_x, piece_v, piece_w, rows_x, rows_v, rows_w, cols_x, cols_v, cols_w,
-           gram, inner, yt, y, y_in, work, load_sem, store_sem, ys, yq, *rest):
+def barrier(w):
+    sem = pltpu.get_barrier_semaphore()
+
+    def greet(row, col):
+        pl.semaphore_signal(sem, inc=1, device_id=(row, col), device_id_type=pl.DeviceIdType.MESH)
+
+    loop(1, 8, lambda d: greet((w.r + d) % 8, w.c))
+    loop(1, 8, lambda d: greet(w.r, w.x * 8 + (w.z + d) % 8))
+    loop(1, 4, lambda d: greet(w.r, (w.x + d) % 4 * 8 + w.z))
+    target = 2 * w.x + w.z // 4
+    loop(1, 4, lambda d: greet(target, (w.x + d) % 4 * 8 + w.z))
+    outside = w.r != target
+
+    @pl.when(outside)
+    def _():
+        greet(target, w.c)
+
+    receives = w.z // 4 == w.k
+
+    @pl.when(receives)
+    def _():
+        def one(owner):
+            @pl.when(jnp.logical_not(jnp.logical_and(owner == w.r, w.x == w.y)))
+            def _():
+                greet(owner, 8 * w.y + w.z)
+        loop(0, 8, one)
+
+    count = 20 + jnp.where(outside, 1, 0) + jnp.where(receives, jnp.where(w.x == w.y, 7, 8), 0)
+    pl.semaphore_wait(sem, count)
+
+
+def split(value):
+    hi = value.astype(BF16)
+    return hi, (value - hi.astype(F32)).astype(BF16)
+
+
+def bdot(left, right, contract=((1,), (0,))):
+    return lax.dot_general(left, right, (contract, ((), ())), preferred_element_type=F32)
+
+
+def kernel(a_hbm, pan, out, a, piece_x, piece_y, rows_x, rows_y, cols_x, cols_y,
+           gram, inner, yt, y, y_in, work, coef, right1, right2, load_sem, store_sem, ys, yq, *rest):
     w = Where()
     n_ar = 16
     ar_g = AllReduce(w, gram, rest[:n_ar])
     ar_s = AllReduce(w, inner, rest[n_ar:2 * n_ar])
     sems = rest[2 * n_ar:]
     g_x = Gather(w, piece_x, rows_x, cols_x, sems[0:6])
-    g_v = Gather(w, piece_v, rows_v, cols_v, sems[6:12])
-    g_w = Gather(w, piece_w, rows_w, cols_w, sems[12:18])
+    g_y = Gather(w, piece_y, rows_y, cols_y, sems[6:12])
 
     load = pltpu.make_async_copy(a_hbm, a, load_sem)
     load.start()
@@ -273,133 +312,146 @@
     p2 = pan[1]
     piece_x[:, 0:NB] = v1.astype(BF16)
     piece_x[:, NB:] = p2.astype(BF16)
+    barrier(w)
     g_x.start()
     both = jnp.concatenate([v1, p2], axis=1)
     gram[0:256] = fdot(both, v1, ((0,), (0,)))
     gram[256:512] = fdot(both, p2, ((0,), (0,)))
     ar_g.step1()
+    yt[...] = jnp.zeros_like(yt)
+
+    def product_block(b):
+        def tile(i):
+            at = pl.ds(pl.multiple_of(b * BLOCK + i * 256, 256), 256)
+            yt[...] += bdot(rows_x[at], a[at], ((0,), (0,)))
+        loop(0, BLOCK // 256, tile)
+
+    def product(t):
+        for way in range(2 if 0 < t < 4 else 1):
+            src_z = (w.z - t + 8) % 8 if way == 0 else (w.z + t) % 8
+
+            @pl.when(src_z // 4 == w.k)
+            def _():
+                product_block(src_z % 4)
+
     g_x.step(0)
     ar_g.step2()
+    load.wait()
+    product(0)
     g_x.step(1)
     ar_g.step3()
+    product(1)
     g_x.step(2)
     ar_g.step4()
+    product(2)
     g_x.step(3)
     ar_g.step5()
+    product(3)
     g_x.step(4)
-    load.wait()
-
-    yt[...] = jnp.zeros_like(yt)
-
-    def product(i):
-        at = pl.ds(pl.multiple_of(i * 256, 256), 256)
-        yt[...] += lax.dot_general(rows_x[at], a[at], (((0,), (0,)), ((), ())), preferred_element_type=F32)
-    loop(0, ROWS // 256, product)
+    product(4)
     y[...] = yt[...].T
-    g_x.wait_cols()
 
     def y_copy(d):
         to = (w.r + d) % 8
         return rcopy(y.at[pl.ds(pl.multiple_of(to * PIECE, PIECE), PIECE)], y_in.at[d - 1],
                      ys.at[d - 1], yq.at[d - 1], to, w.c)
 
-    hi = yt[...].astype(BF16)
-    lo = (yt[...] - hi.astype(F32)).astype(BF16)
-    s_t = (lax.dot_general(hi, cols_x[...], (((1,), (0,)), ((), ())), preferred_element_type=F32)
-           + lax.dot_general(lo, cols_x[...], (((1,), (0,)), ((), ())), preferred_element_type=F32))
+    loop(1, 8, lambda d: y_copy(d).start())
+    g_x.wait_cols()
+    hi, lo = split(yt[...])
+    s_t = bdot(hi, cols_x[...]) + bdot(lo, cols_x[...])
     inner[0:256] = s_t[:, 0:NB]
     inner[256:512] = s_t[:, NB:]
     ar_s.step1()
-    loop(1, 8, lambda d: y_copy(d).start())
 
     ar_g.finish()
-    g1 = ar_g.out[0:128]
     cross = ar_g.out[256:384]
-    g2 = ar_g.out[384:512]
     eye2 = jnp.where(lax.broadcasted_iota(jnp.int32, (NB, NB), 0) == lax.broadcasted_iota(jnp.int32, (NB, NB), 1),
                      2.0, 0.0).astype(F32)
-    work[0, :, 0:NB] = g1
-    work[1, :, 0:NB] = g2
+    work[0, :, 0:NB] = ar_g.out[0:128]
+    work[1, :, 0:NB] = ar_g.out[384:512]
     work[0, :, NB:] = eye2
     work[1, :, NB:] = eye2
-    invert(work, 0, 4)
+    invert(work, 0, 6)
     ar_s.step2()
-    invert(work, 4, 8)
+    invert(work, 6, 12)
     ar_s.step3()
-    invert(work, 8, 12)
-    ar_s.step4()
-    invert(work, 12, 16)
-    ar_s.step5()
-    f1 = work[0, :, NB:]
-    f2 = work[1, :, NB:]
-    mix = fdot(f1, cross)
-    v2 = p2 - fdot(v1, mix)
-    piece_v[...] = v2.astype(BF16)
-    g_v.start()
-
     loop(1, 8, lambda d: y_copy(d).wait_recv())
     total = y[pl.ds(pl.multiple_of(w.r * PIECE, PIECE), PIECE)]
     for d in range(7):
         total = total + y_in[d]
-    y1 = total[:, 0:NB]
-    y2 = total[:, NB:] - fdot(y1, mix)
+    piece_y[...] = total.astype(BF16)
+    g_y.start()
+    invert(work, 12, 16)
+    ar_s.step4()
+    g_y.step(0)
+    f1 = work[0, :, NB:]
+    f2 = work[1, :, NB:]
+    mix = fdot(f1, cross)
+    mix2 = fdot(cross, f2)
+    ar_s.step5()
+    g_y.step(1)
     ar_s.finish()
-    g_v.step(0)
     s11 = ar_s.out[0:128]
     s21 = ar_s.out[128:256]
     s12 = ar_s.out[256:384]
     s22 = ar_s.out[384:512]
-    tt = (((0,), (0,)))
+    tt = ((0,), (0,))
     b12 = s12 - fdot(s11, mix)
-    b21 = s21 - fdot(mix, s11, tt)
     b22 = s22 - fdot(s21, mix) - fdot(mix, b12, tt)
-    k1 = fdot(s11, f1, tt)
-    l1 = 0.5 * fdot(f1, k1)
-    g_v.step(1)
+    l1 = 0.5 * fdot(f1, fdot(s11, f1, tt))
     h = fdot(f1, b12, tt) + fdot(l1, cross, tt)
+    g_y.step(2)
     hc = fdot(h, cross, tt)
-    k2 = fdot(b22.T + hc + hc.T, f2)
-    l2 = 0.5 * fdot(f2, k2)
-    w1 = fdot(y1, f1) - fdot(v1, l1)
-    prod2 = y2 + fdot(w1, cross) - fdot(v1, h)
-    w2 = fdot(prod2, f2) - fdot(v2, l2)
-    piece_w[:, 0:NB] = w1.astype(BF16)
-    piece_w[:, NB:] = w2.astype(BF16)
-    g_w.start()
-    g_v.step(2)
-    g_w.step(0)
-    g_v.step(3)
-    g_w.step(1)
-    g_v.step(4)
-    g_w.step(2)
-    g_w.step(3)
-    g_w.step(4)
-    g_v.wait_cols()
-    g_w.wait_cols()
+    l2 = 0.5 * fdot(f2, fdot(b22.T + hc + hc.T, f2))
+    b = fdot(mix, l2) - (fdot(l1, mix2) + fdot(h, f2))
+    for n, part in enumerate((f1, -l1, f2, b, -l2, -mix)):
+        hi, lo = split(part)
+        coef[n, 0] = hi
+        coef[n, 1] = lo
+    g_y.step(3)
+    g_y.step(4)
+    g_y.wait_cols()
+
+    def times(left, n):
+        return bdot(left, coef[n, 0]) + bdot(left, coef[n, 1])
+
+    def form(x_ref, y_ref, at):
+        v1b = x_ref[at, 0:NB]
+        p2b = x_ref[at, NB:]
+        w1 = times(y_ref[at, 0:NB], 0) + times(v1b, 1)
+        w2 = times(y_ref[at, NB:], 2) + times(v1b, 3) + times(p2b, 4)
+        v2 = p2b.astype(F32) + times(v1b, 5)
+        return v1b, w1.astype(BF16), v2.astype(BF16), w2.astype(BF16)
+
+    def right(i):
+        at = pl.ds(pl.multiple_of(i * 256, 256), 256)
+        v1b, w1, v2, w2 = form(cols_x, cols_y, at)
+        right1[at, 0:NB] = w1
+        right1[at, NB:] = v1b
+        right2[at, 0:NB] = w2
+        right2[at, NB:] = v2
+    loop(0, BLOCK // 256, right)
 
     def store(i):
         at = pl.ds(pl.multiple_of(i * 256, 256), 256)
         return pltpu.make_async_copy(a.at[at], out.at[at], store_sem.at[i])
 
-    right1 = jnp.concatenate([cols_w[:, 0:NB], cols_x[:, 0:NB]], axis=1)
-    right2 = jnp.concatenate([cols_w[:, NB:], cols_v[...]], axis=1)
-
     def update(i):
         at = pl.ds(pl.multiple_of(i * 256, 256), 256)
-        nt = (((1,), (1,)), ((), ()))
-        left1 = jnp.concatenate([rows_x[at, 0:NB], rows_w[at, 0:NB]], axis=1)
-        left2 = jnp.concatenate([rows_v[at, :], rows_w[at, NB:]], axis=1)
-        one = (a[at].astype(F32) - lax.dot_general(left1, right1, nt, preferred_element_type=F32)).astype(BF16)
-        two = one.astype(F32) - lax.dot_general(left2, right2, nt, preferred_element_type=F32)
-        a[at] = two.astype(BF16)
+        nt = ((1,), (1,))
+        v1b, w1, v2, w2 = form(rows_x, rows_y, at)
+        left1 = jnp.concatenate([v1b, w1], axis=1)
+        left2 = jnp.concatenate([v2, w2], axis=1)
+        one = (a[at].astype(F32) - bdot(left1, right1[...], nt)).astype(BF16)
+        a[at] = (one.astype(F32) - bdot(left2, right2[...], nt)).astype(BF16)
         store(i).start()
     loop(0, ROWS // 256, update)
 
     ar_g.drain()
     ar_s.drain()
     g_x.drain()
-    g_v.drain()
-    g_w.drain()
+    g_y.drain()
     loop(1, 8, lambda d: y_copy(d).wait_send())
     loop(0, ROWS // 256, lambda i: store(i).wait())
 
@@ -409,12 +461,13 @@
     dma = pltpu.SemaphoreType.DMA
     shapes = [
         vm((ROWS, BLOCK), BF16),
-        vm((PIECE, 256), BF16), vm((PIECE, 128), BF16), vm((PIECE, 256), BF16),
-        vm((ROWS, 256), BF16), vm((ROWS, 128), BF16), vm((ROWS, 256), BF16),
-        vm((BLOCK, 256), BF16), vm((BLOCK, 128), BF16), vm((BLOCK, 256), BF16),
+        vm((PIECE, 256), BF16), vm((PIECE, 256), BF16),
+        vm((ROWS, 256), BF16), vm((ROWS, 256), BF16),
+        vm((BLOCK, 256), BF16), vm((BLOCK, 256), BF16),
         vm((512, 128), F32), vm((512, 128), F32),
         vm((256, BLOCK), F32), vm((BLOCK, 256), F32), vm((7, PIECE, 256), F32),
         vm((2, NB, 2 * NB), F32),
+        vm((6, 2, NB, NB), BF16), vm((BLOCK, 256), BF16), vm((BLOCK, 256), BF16),
         dma(()), dma((ROWS // 256,)), dma((7,)), dma((7,)),
     ]
     for _ in range(2):
@@ -423,7 +476,7 @@
             vm((64, 128), F32), vm((512, 128), F32),
             dma((7,)), dma((7,)), dma((7,)), dma((7,)), dma((3,)), dma((3,)), dma((7,)), dma((7,)), dma((7,)), dma((7,)),
         ]
-    for _ in range(3):
+    for _ in range(2):
         shapes += [dma((7,)), dma((7,)), dma((4,)), dma((8,)), dma((2, 4)), dma((2, 4))]
     return shapes
 
@@ -435,7 +488,7 @@
         in_specs=[pl.BlockSpec(memory_space=pl.ANY), pl.BlockSpec(memory_space=pltpu.VMEM)],
         out_specs=pl.BlockSpec(memory_space=pl.ANY),
         scratch_shapes=scratch(),
-        compiler_params=pltpu.CompilerParams(has_side_effects=True, vmem_limit_bytes=48 * 1024 * 1024),
+        compiler_params=pltpu.CompilerParams(collective_id=0, has_side_effects=True, vmem_limit_bytes=48 * 1024 * 1024),
         cost_estimate=pl.CostEstimate(flops=3700000000, bytes_accessed=9437184, transcendentals=0),
     )(matrix, panels)
 

time: 135 us -> 112 us (0.83)
  Pallas kernels: 132 us -> 109 us
    pallas_call x1, Pallas kernels: 132 us -> 109 us  [per_device(): pl.pallas_call(kernel, out_shape=jax.ShapeDtypeStruct((ROWS, BLOCK), BF16...]
where the time goes in v2:
time: 112 us
  Pallas kernels  109 us (97%)
  local copies, waits for them, and re-layouts  3.08 us (3%)
    pallas_call x1, Pallas kernels, per_device(): pl.pallas_call(kernel, out_shape=jax.ShapeDtypeStruct((ROWS, BLOCK), BF16...  109 us
    unnamed x3, local copies, waits for them, and re-layouts  3.08 us

profile of v2, /device:TPU:1, one launch (start us, length us, event | category | flops | bytes accessed | tf_op | source)
XLA Modules:
  0.0 111.8 jit_solution(4464272650129326801)
XLA Ops:
  0.0 0.0 copy-start
  0.0 0.9 copy-done
  0.9 108.7 %shard_map.28 = bf16[3072,768]{1,0:T(8,128)(2,1)S(1)} custom-call(bf16[3072,768]{1,0:T(8,128)(2,1)} %a_hbm.1, f32[2,96,128]{2,1,0:T(8,128)S(1)} %copy-done), custom_call_target="tpu_custom_call" | custom-call | flops 3700000000 | bytes 9437184 | tf_op jit(solution)/shard_map/pallas_call | solution.py:485
  109.6 2.2 %copy.4 = bf16[3072,768]{1,0:T(8,128)(2,1)} copy(bf16[3072,768]{1,0:T(8,128)(2,1)S(1)} %shard_map.28) | data formatting | bytes 9437184
Async XLA Ops:
  0.0 0.9 copy-start

commit v3 on v2

--- a/solution.py
+++ b/solution.py
@@ -60,20 +60,20 @@
 
     def copy2(self, d):
         w = self.w
+        to = (w.x + d) % 4
+        return rcopy(self.acc.at[pl.ds(pl.multiple_of(to * 16, 16), 16)], self.in2.at[d - 1],
+                     self.s2.at[d - 1], self.q2.at[d - 1], w.r, to * 8 + w.z)
+
+    def copy3(self, d, slot):
+        w = self.w
         to = (w.z + d) % 8
-        return rcopy(self.acc.at[pl.ds(pl.multiple_of(to * 8, 8), 8)], self.in2.at[d - 1],
-                     self.s2.at[d - 1], self.q2.at[d - 1], w.r, w.x * 8 + to)
-
-    def copy3(self, d):
+        return rcopy(self.in3.at[slot], self.in3.at[slot], self.s3.at[d - 1], self.q3.at[d - 1], w.r, w.x * 8 + to)
+
+    def copy4(self, d, owner):
         w = self.w
         to = (w.x + d) % 4
-        return rcopy(self.in3.at[0], self.in3.at[d], self.s3.at[d - 1], self.q3.at[d - 1], w.r, to * 8 + w.z)
-
-    def copy4(self, d, owner):
-        w = self.w
-        to = (w.z + d) % 8
-        part = self.g4.at[pl.ds(pl.multiple_of(owner * 8, 8), 8)]
-        return rcopy(part, part, self.s4.at[d - 1], self.q4.at[d - 1], w.r, w.x * 8 + to)
+        part = self.g4.at[pl.ds(pl.multiple_of(owner * 16, 16), 16)]
+        return rcopy(part, part, self.s4.at[d - 1], self.q4.at[d - 1], w.r, to * 8 + w.z)
 
     def copy5(self, d, owner):
         w = self.w
@@ -90,26 +90,29 @@
         for d in range(7):
             total = total + self.in1[d]
         self.acc[...] = total
-        loop(1, 8, lambda d: self.copy2(d).start())
+        loop(1, 4, lambda d: self.copy2(d).start())
 
     def step3(self):
-        loop(1, 8, lambda d: self.copy2(d).wait_recv())
-        total = self.acc[pl.ds(pl.multiple_of(self.w.z * 8, 8), 8)]
-        for d in range(7):
+        w = self.w
+        loop(1, 4, lambda d: self.copy2(d).wait_recv())
+        total = self.acc[pl.ds(pl.multiple_of(w.x * 16, 16), 16)]
+        for d in range(3):
             total = total + self.in2[d]
-        self.in3[0] = total
-        loop(1, 4, lambda d: self.copy3(d).start())
+        self.in3[w.z] = total
+        loop(1, 8, lambda d: self.copy3(d, w.z).start())
 
     def step4(self):
-        z = self.w.z
-        loop(1, 4, lambda d: self.copy3(d).wait_recv())
-        total = (self.in3[0] + self.in3[2]) + (self.in3[1] + self.in3[3])
-        self.g4[pl.ds(pl.multiple_of(z * 8, 8), 8)] = total
-        loop(1, 8, lambda d: self.copy4(d, z).start())
+        w = self.w
+        loop(1, 8, lambda d: self.copy3(d, (w.z - d + 8) % 8).wait_recv())
+        total = self.in3[0]
+        for d in range(1, 8):
+            total = total + self.in3[d]
+        self.g4[pl.ds(pl.multiple_of(w.x * 16, 16), 16)] = total
+        loop(1, 4, lambda d: self.copy4(d, w.x).start())
 
     def step5(self):
         w = self.w
-        loop(1, 8, lambda d: self.copy4(d, (w.z - d + 8) % 8).wait_recv())
+        loop(1, 4, lambda d: self.copy4(d, (w.x - d + 4) % 4).wait_recv())
         self.out[pl.ds(pl.multiple_of(w.r * 64, 64), 64)] = self.g4[...]
         loop(1, 8, lambda d: self.copy5(d, w.r).start())
 
@@ -120,9 +123,9 @@
     def drain(self):
         w = self.w
         loop(1, 8, lambda d: self.copy1(d).wait_send())
-        loop(1, 8, lambda d: self.copy2(d).wait_send())
-        loop(1, 4, lambda d: self.copy3(d).wait_send())
-        loop(1, 8, lambda d: self.copy4(d, w.z).wait_send())
+        loop(1, 4, lambda d: self.copy2(d).wait_send())
+        loop(1, 8, lambda d: self.copy3(d, w.z).wait_send())
+        loop(1, 4, lambda d: self.copy4(d, w.x).wait_send())
         loop(1, 8, lambda d: self.copy5(d, w.r).wait_send())
 
 
@@ -145,17 +148,13 @@
         return rcopy(self.piece, self.rows.at[pl.ds(at, PIECE)], self.xs.at[d], self.xq.at[owner],
                      2 * w.x + w.z // 4, ((w.x + d) % 4) * 8 + w.z)
 
-    def z_copy(self, way, t, at_z):
+    def z_copy(self, way, t, half, at_z):
         w = self.w
         src_z = (at_z - t + 8) % 8 if way == 0 else (at_z + t) % 8
-        base = (src_z % 4) * BLOCK
-        if t < 3:
-            part = self.rows.at[pl.ds(pl.multiple_of(base, BLOCK), BLOCK)]
-        else:
-            half = BLOCK // 2
-            part = self.rows.at[pl.ds(pl.multiple_of(base + way * half, half), half)]
+        rows = BLOCK // 2
+        part = self.rows.at[pl.ds(pl.multiple_of((src_z % 4) * BLOCK + half * rows, rows), rows)]
         to = (w.z + 1) % 8 if way == 0 else (w.z + 7) % 8
-        copy = rcopy(part, part, self.zs.at[way, t], self.zq.at[way, t], w.r, w.x * 8 + to)
+        copy = rcopy(part, part, self.zs.at[way, t, half], self.zq.at[way, t, half], w.r, w.x * 8 + to)
         return copy, src_z // 4 == w.k
 
     def start(self):
@@ -187,30 +186,28 @@
                     self.x_copy(0, owner).wait_recv()
             loop(0, 8, one)
 
-    def send_z(self, t):
-        for way in range(2):
-            copy, mine = self.z_copy(way, t, self.w.z)
-
-            @pl.when(mine)
-            def _():
-                copy.start()
-
-    def wait_z(self, t):
+    def halves(self, t):
+        if t == 3:
+            return ((0, 0), (1, 1))
+        return ((0, 0), (1, 1), (0, 1), (1, 0))
+
+    def step(self, t):
         z = self.w.z
-        for way in range(2):
-            copy, mine = self.z_copy(way, t, (z + 7) % 8 if way == 0 else (z + 1) % 8)
-
-            @pl.when(mine)
-            def _():
-                copy.wait_recv()
-
-    def step(self, t):
         if t == 0:
             self.wait_x()
-        else:
-            self.wait_z(t - 1)
-        if t < 4:
-            self.send_z(t)
+        for way, half in self.halves(max(t - 1, 0)):
+            if t > 0:
+                copy, mine = self.z_copy(way, t - 1, half, (z + 7) % 8 if way == 0 else (z + 1) % 8)
+
+                @pl.when(mine)
+                def _():
+                    copy.wait_recv()
+            if t < 4 and (way, half) in self.halves(t):
+                copy, mine = self.z_copy(way, t, half, z)
+
+                @pl.when(mine)
+                def _():
+                    copy.start()
 
     def wait_cols(self):
         w = self.w
@@ -227,8 +224,8 @@
 
         loop(1, 8, lambda d: self.col_copy(d, w.r).wait_send())
         for t in range(4):
-            for way in range(2):
-                copy, mine = self.z_copy(way, t, w.z)
+            for way, half in self.halves(t):
+                copy, mine = self.z_copy(way, t, half, w.z)
 
                 @pl.when(mine)
                 def _():
@@ -236,23 +233,28 @@
 
 
 def invert(work, lo, hi):
-    sub = lax.broadcasted_iota(jnp.int32, (8, 2 * NB), 0)
+    sub = lax.broadcasted_iota(jnp.int32, (8, NB), 0)
+    lane = lax.broadcasted_iota(jnp.int32, (8, NB), 1)
+    lanes = lax.broadcasted_iota(jnp.int32, (NB, NB), 1)
+    both = range(2)
 
     def panel(p):
-        at = pl.multiple_of(p * 8, 8)
-        for m in range(2):
-            rows = work[m, pl.ds(at, 8), :]
-            for j in range(8):
-                pivot = rows[j:j + 1, :] / rows[j:j + 1, j:j + 1]
-                rows = jnp.where(sub == j, pivot, rows - rows[:, j:j + 1] * pivot)
-            whole = work[m]
-            new = whole
-            for j in range(8):
-                new = new - whole[:, j:j + 1] * rows[j:j + 1, :]
-            work[m, :, 0:NB] = pltpu.roll(new[:, :NB], NB - 8, 1)
-            work[m, :, NB:] = new[:, NB:]
-            work[m, pl.ds(at, 8), 0:NB] = pltpu.roll(rows[:, :NB], NB - 8, 1)
-            work[m, pl.ds(at, 8), NB:] = rows[:, NB:]
+        at = pl.ds(pl.multiple_of(p * 8, 8), 8)
+        rows = [work[m, at, :] for m in both]
+        whole = [work[m] for m in both]
+        for j in range(8):
+            for m in both:
+                column = jnp.broadcast_to(rows[m][:, j:j + 1], (8, NB))
+                rest = jnp.where(lane == j, jnp.where(sub == j, 1.0, 0.0), rows[m])
+                pivot = rest[j:j + 1, :] * (1.0 / column[j:j + 1, :])
+                rows[m] = jnp.where(sub == j, pivot, rest - column * pivot)
+        new = [jnp.where(lanes < 8, 0.0, whole[m]) for m in both]
+        for j in range(8):
+            for m in both:
+                new[m] = new[m] - whole[m][:, j:j + 1] * rows[m][j:j + 1, :]
+        for m in both:
+            work[m] = pltpu.roll(new[m], NB - 8, 1)
+            work[m, at, :] = pltpu.roll(rows[m], NB - 8, 1)
     loop(lo, hi, panel)
 
 
@@ -297,7 +299,7 @@
 
 
 def kernel(a_hbm, pan, out, a, piece_x, piece_y, rows_x, rows_y, cols_x, cols_y,
-           gram, inner, yt, y, y_in, work, coef, right1, right2, load_sem, store_sem, ys, yq, *rest):
+           gram, inner, yt, y, y_in, work, coef_x, coef_y, right1, right2, load_sem, store_sem, ys, yq, *rest):
     w = Where()
     n_ar = 16
     ar_g = AllReduce(w, gram, rest[:n_ar])
@@ -326,13 +328,16 @@
             yt[...] += bdot(rows_x[at], a[at], ((0,), (0,)))
         loop(0, BLOCK // 256, tile)
 
-    def product(t):
+    def by_step(t, body):
         for way in range(2 if 0 < t < 4 else 1):
             src_z = (w.z - t + 8) % 8 if way == 0 else (w.z + t) % 8
 
             @pl.when(src_z // 4 == w.k)
             def _():
-                product_block(src_z % 4)
+                body(src_z % 4)
+
+    def product(t):
+        by_step(t, product_block)
 
     g_x.step(0)
     ar_g.step2()
@@ -349,7 +354,7 @@
     product(3)
     g_x.step(4)
     product(4)
-    y[...] = yt[...].T
+    y[...] = yt[...].T.astype(BF16)
 
     def y_copy(d):
         to = (w.r + d) % 8
@@ -366,31 +371,32 @@
 
     ar_g.finish()
     cross = ar_g.out[256:384]
-    eye2 = jnp.where(lax.broadcasted_iota(jnp.int32, (NB, NB), 0) == lax.broadcasted_iota(jnp.int32, (NB, NB), 1),
-                     2.0, 0.0).astype(F32)
-    work[0, :, 0:NB] = ar_g.out[0:128]
-    work[1, :, 0:NB] = ar_g.out[384:512]
-    work[0, :, NB:] = eye2
-    work[1, :, NB:] = eye2
-    invert(work, 0, 6)
-    ar_s.step2()
-    invert(work, 6, 12)
-    ar_s.step3()
+    eye = jnp.where(lax.broadcasted_iota(jnp.int32, (NB, NB), 0) == lax.broadcasted_iota(jnp.int32, (NB, NB), 1),
+                    1.0, 0.0).astype(F32)
+    work[0] = ar_g.out[0:128]
+    work[1] = ar_g.out[384:512]
+    invert(work, 0, 5)
     loop(1, 8, lambda d: y_copy(d).wait_recv())
-    total = y[pl.ds(pl.multiple_of(w.r * PIECE, PIECE), PIECE)]
+    total = y[pl.ds(pl.multiple_of(w.r * PIECE, PIECE), PIECE)].astype(F32)
     for d in range(7):
-        total = total + y_in[d]
+        total = total + y_in[d].astype(F32)
     piece_y[...] = total.astype(BF16)
     g_y.start()
-    invert(work, 12, 16)
+    ar_s.step2()
+    invert(work, 5, 8)
+    ar_s.step3()
+    invert(work, 8, 11)
+    g_y.step(0)
+    invert(work, 11, 14)
     ar_s.step4()
-    g_y.step(0)
-    f1 = work[0, :, NB:]
-    f2 = work[1, :, NB:]
+    g_y.step(1)
+    invert(work, 14, 16)
+    f1 = 2.0 * work[0]
+    f2 = 2.0 * work[1]
     mix = fdot(f1, cross)
     mix2 = fdot(cross, f2)
     ar_s.step5()
-    g_y.step(1)
+    g_y.step(2)
     ar_s.finish()
     s11 = ar_s.out[0:128]
     s21 = ar_s.out[128:256]
@@ -401,52 +407,56 @@
     b22 = s22 - fdot(s21, mix) - fdot(mix, b12, tt)
     l1 = 0.5 * fdot(f1, fdot(s11, f1, tt))
     h = fdot(f1, b12, tt) + fdot(l1, cross, tt)
-    g_y.step(2)
     hc = fdot(h, cross, tt)
     l2 = 0.5 * fdot(f2, fdot(b22.T + hc + hc.T, f2))
     b = fdot(mix, l2) - (fdot(l1, mix2) + fdot(h, f2))
-    for n, part in enumerate((f1, -l1, f2, b, -l2, -mix)):
-        hi, lo = split(part)
-        coef[n, 0] = hi
-        coef[n, 1] = lo
+    zero = jnp.zeros((NB, NB), F32)
+    for at, parts in ((coef_y, ((f1, zero), (zero, f2))), (coef_x, ((-l1, b, -mix), (zero, -l2, eye)))):
+        for i, line in enumerate(parts):
+            for j, part in enumerate(line):
+                hi, lo = split(part)
+                at[0, i * NB:(i + 1) * NB, j * NB:(j + 1) * NB] = hi
+                at[1, i * NB:(i + 1) * NB, j * NB:(j + 1) * NB] = lo
     g_y.step(3)
-    g_y.step(4)
     g_y.wait_cols()
 
-    def times(left, n):
-        return bdot(left, coef[n, 0]) + bdot(left, coef[n, 1])
-
     def form(x_ref, y_ref, at):
-        v1b = x_ref[at, 0:NB]
-        p2b = x_ref[at, NB:]
-        w1 = times(y_ref[at, 0:NB], 0) + times(v1b, 1)
-        w2 = times(y_ref[at, NB:], 2) + times(v1b, 3) + times(p2b, 4)
-        v2 = p2b.astype(F32) + times(v1b, 5)
-        return v1b, w1.astype(BF16), v2.astype(BF16), w2.astype(BF16)
-
-    def right(i):
-        at = pl.ds(pl.multiple_of(i * 256, 256), 256)
+        xt = x_ref[at]
+        yy = y_ref[at]
+        both_x = bdot(xt, coef_x[0]) + bdot(xt, coef_x[1])
+        wide = both_x[:, 0:2 * NB] + bdot(yy, coef_y[0]) + bdot(yy, coef_y[1])
+        wb = wide.astype(BF16)
+        return xt[:, 0:NB], wb[:, 0:NB], both_x[:, 2 * NB:].astype(BF16), wb[:, NB:]
+
+    for i in range(BLOCK // 256):
+        at = slice(i * 256, (i + 1) * 256)
         v1b, w1, v2, w2 = form(cols_x, cols_y, at)
-        right1[at, 0:NB] = w1
-        right1[at, NB:] = v1b
-        right2[at, 0:NB] = w2
-        right2[at, NB:] = v2
-    loop(0, BLOCK // 256, right)
+        right1[0:NB, at] = w1.T
+        right1[NB:, at] = v1b.T
+        right2[0:NB, at] = w2.T
+        right2[NB:, at] = v2.T
 
     def store(i):
         at = pl.ds(pl.multiple_of(i * 256, 256), 256)
         return pltpu.make_async_copy(a.at[at], out.at[at], store_sem.at[i])
 
-    def update(i):
-        at = pl.ds(pl.multiple_of(i * 256, 256), 256)
-        nt = ((1,), (1,))
-        v1b, w1, v2, w2 = form(rows_x, rows_y, at)
-        left1 = jnp.concatenate([v1b, w1], axis=1)
-        left2 = jnp.concatenate([v2, w2], axis=1)
-        one = (a[at].astype(F32) - bdot(left1, right1[...], nt)).astype(BF16)
-        a[at] = (one.astype(F32) - bdot(left2, right2[...], nt)).astype(BF16)
-        store(i).start()
-    loop(0, ROWS // 256, update)
+    def update_block(block):
+        for i in range(BLOCK // 256):
+            at = pl.ds(pl.multiple_of(block * BLOCK + i * 256, 256), 256)
+            v1b, w1, v2, w2 = form(rows_x, rows_y, at)
+            left1 = jnp.concatenate([v1b, w1], axis=1)
+            left2 = jnp.concatenate([v2, w2], axis=1)
+            one = (a[at].astype(F32) - bdot(left1, right1[...])).astype(BF16)
+            a[at] = (one.astype(F32) - bdot(left2, right2[...])).astype(BF16)
+            store(block * (BLOCK // 256) + i).start()
+
+    def update(t):
+        by_step(t, update_block)
+
+    for t in range(4):
+        update(t)
+    g_y.step(4)
+    update(4)
 
     ar_g.drain()
     ar_s.drain()
@@ -465,19 +475,19 @@
         vm((ROWS, 256), BF16), vm((ROWS, 256), BF16),
         vm((BLOCK, 256), BF16), vm((BLOCK, 256), BF16),
         vm((512, 128), F32), vm((512, 128), F32),
-        vm((256, BLOCK), F32), vm((BLOCK, 256), F32), vm((7, PIECE, 256), F32),
-        vm((2, NB, 2 * NB), F32),
-        vm((6, 2, NB, NB), BF16), vm((BLOCK, 256), BF16), vm((BLOCK, 256), BF16),
+        vm((256, BLOCK), F32), vm((BLOCK, 256), BF16), vm((7, PIECE, 256), BF16),
+        vm((2, NB, NB), F32),
+        vm((2, 2 * NB, 3 * NB), BF16), vm((2, 2 * NB, 2 * NB), BF16), vm((256, BLOCK), BF16), vm((256, BLOCK), BF16),
         dma(()), dma((ROWS // 256,)), dma((7,)), dma((7,)),
     ]
     for _ in range(2):
         shapes += [
-            vm((7, 64, 128), F32), vm((64, 128), F32), vm((7, 8, 128), F32), vm((4, 8, 128), F32),
+            vm((7, 64, 128), F32), vm((64, 128), F32), vm((3, 16, 128), F32), vm((8, 16, 128), F32),
             vm((64, 128), F32), vm((512, 128), F32),
-            dma((7,)), dma((7,)), dma((7,)), dma((7,)), dma((3,)), dma((3,)), dma((7,)), dma((7,)), dma((7,)), dma((7,)),
+            dma((7,)), dma((7,)), dma((3,)), dma((3,)), dma((7,)), dma((7,)), dma((3,)), dma((3,)), dma((7,)), dma((7,)),
         ]
     for _ in range(2):
-        shapes += [dma((7,)), dma((7,)), dma((4,)), dma((8,)), dma((2, 4)), dma((2, 4))]
+        shapes += [dma((7,)), dma((7,)), dma((4,)), dma((8,)), dma((2, 4, 2)), dma((2, 4, 2))]
     return shapes
 
 

time: 112 us -> 96.6 us (0.86)
  the two profiles are of different devices: /device:TPU:1 before, /device:TPU:0 now
where the time goes in v3:
time: 96.6 us; the launch traced here: 96.5 us
  Pallas kernels  93.4 us (97%)
  local copies, waits for them, and re-layouts  3.08 us (3%)
    pallas_call x1, Pallas kernels, per_device(): pl.pallas_call(kernel, out_shape=jax.ShapeDtypeStruct((ROWS, BLOCK), BF16...  93.4 us
    unnamed x3, local copies, waits for them, and re-layouts  3.08 us

profile of v3, /device:TPU:0, one launch (start us, length us, event | category | flops | bytes accessed | tf_op | source)
XLA Modules:
  0.0 96.5 jit_solution(9546686147816186941)
XLA Ops:
  0.0 0.0 copy-start
  0.0 0.9 copy-done
  0.9 93.4 %shard_map.28 = bf16[3072,768]{1,0:T(8,128)(2,1)S(1)} custom-call(bf16[3072,768]{1,0:T(8,128)(2,1)} %a_hbm.1, f32[2,96,128]{2,1,0:T(8,128)S(1)} %copy-done), custom_call_target="tpu_custom_call" | custom-call | flops 3700000000 | bytes 9437184 | tf_op jit(solution)/shard_map/pallas_call | solution.py:495
  94.3 2.2 %copy.4 = bf16[3072,768]{1,0:T(8,128)(2,1)} copy(bf16[3072,768]{1,0:T(8,128)(2,1)S(1)} %shard_map.28) | data formatting | bytes 9437184
Async XLA Ops:
  0.0 0.9 copy-start

commit v4 on v3

--- a/solution.py
+++ b/solution.py
@@ -172,6 +172,8 @@
             at = pl.multiple_of((w.z % 4) * BLOCK + w.r * PIECE, PIECE)
             self.rows[pl.ds(at, PIECE)] = self.piece[...]
 
+    def start_cols(self):
+        w = self.w
         loop(1, 8, lambda d: self.col_copy(d, w.r).start())
         self.cols[pl.ds(pl.multiple_of(w.r * PIECE, PIECE), PIECE)] = self.piece[...]
 
@@ -299,7 +301,7 @@
 
 
 def kernel(a_hbm, pan, out, a, piece_x, piece_y, rows_x, rows_y, cols_x, cols_y,
-           gram, inner, yt, y, y_in, work, coef_x, coef_y, right1, right2, load_sem, store_sem, ys, yq, *rest):
+           gram, inner, yt, y, y_in, work, coef_x, coef_y, right1, right2, left, load_sem, store_sem, ys, yq, *rest):
     w = Where()
     n_ar = 16
     ar_g = AllReduce(w, gram, rest[:n_ar])
@@ -340,6 +342,7 @@
         by_step(t, product_block)
 
     g_x.step(0)
+    g_x.start_cols()
     ar_g.step2()
     load.wait()
     product(0)
@@ -387,6 +390,7 @@
     ar_s.step3()
     invert(work, 8, 11)
     g_y.step(0)
+    g_y.start_cols()
     invert(work, 11, 14)
     ar_s.step4()
     g_y.step(1)
@@ -411,44 +415,47 @@
     l2 = 0.5 * fdot(f2, fdot(b22.T + hc + hc.T, f2))
     b = fdot(mix, l2) - (fdot(l1, mix2) + fdot(h, f2))
     zero = jnp.zeros((NB, NB), F32)
-    for at, parts in ((coef_y, ((f1, zero), (zero, f2))), (coef_x, ((-l1, b, -mix), (zero, -l2, eye)))):
-        for i, line in enumerate(parts):
-            for j, part in enumerate(line):
-                hi, lo = split(part)
-                at[0, i * NB:(i + 1) * NB, j * NB:(j + 1) * NB] = hi
-                at[1, i * NB:(i + 1) * NB, j * NB:(j + 1) * NB] = lo
+    for i, line in enumerate(((f1, zero), (zero, f2))):
+        for j, part in enumerate(line):
+            hi, lo = split(part)
+            coef_y[0, i * NB:(i + 1) * NB, j * NB:(j + 1) * NB] = hi
+            coef_y[1, i * NB:(i + 1) * NB, j * NB:(j + 1) * NB] = lo
+    for i, line in enumerate(((-l1, b, -mix), (zero, -l2, eye))):
+        for j, part in enumerate(line):
+            coef_x[i * NB:(i + 1) * NB, j * NB:(j + 1) * NB] = part.astype(BF16)
     g_y.step(3)
     g_y.wait_cols()
 
     def form(x_ref, y_ref, at):
         xt = x_ref[at]
         yy = y_ref[at]
-        both_x = bdot(xt, coef_x[0]) + bdot(xt, coef_x[1])
+        both_x = bdot(xt, coef_x[...])
         wide = both_x[:, 0:2 * NB] + bdot(yy, coef_y[0]) + bdot(yy, coef_y[1])
         wb = wide.astype(BF16)
         return xt[:, 0:NB], wb[:, 0:NB], both_x[:, 2 * NB:].astype(BF16), wb[:, NB:]
 
-    for i in range(BLOCK // 256):
-        at = slice(i * 256, (i + 1) * 256)
-        v1b, w1, v2, w2 = form(cols_x, cols_y, at)
-        right1[0:NB, at] = w1.T
-        right1[NB:, at] = v1b.T
-        right2[0:NB, at] = w2.T
-        right2[NB:, at] = v2.T
+    v1b, w1, v2, w2 = form(cols_x, cols_y, slice(0, BLOCK))
+    right1[0:NB] = w1.T
+    right1[NB:] = v1b.T
+    right2[0:NB] = w2.T
+    right2[NB:] = v2.T
 
     def store(i):
-        at = pl.ds(pl.multiple_of(i * 256, 256), 256)
+        at = pl.ds(pl.multiple_of(i * BLOCK, BLOCK), BLOCK)
         return pltpu.make_async_copy(a.at[at], out.at[at], store_sem.at[i])
 
     def update_block(block):
-        for i in range(BLOCK // 256):
-            at = pl.ds(pl.multiple_of(block * BLOCK + i * 256, 256), 256)
-            v1b, w1, v2, w2 = form(rows_x, rows_y, at)
-            left1 = jnp.concatenate([v1b, w1], axis=1)
-            left2 = jnp.concatenate([v2, w2], axis=1)
-            one = (a[at].astype(F32) - bdot(left1, right1[...])).astype(BF16)
-            a[at] = (one.astype(F32) - bdot(left2, right2[...])).astype(BF16)
-            store(block * (BLOCK // 256) + i).start()
+        at = pl.ds(pl.multiple_of(block * BLOCK, BLOCK), BLOCK)
+        v1b, w1, v2, w2 = form(rows_x, rows_y, at)
+        left[0, :, 0:NB] = v1b
+        left[0, :, NB:] = w1
+        left[1, :, 0:NB] = v2
+        left[1, :, NB:] = w2
+        for n in range(BLOCK // 256):
+            cut = slice(n * 256, (n + 1) * 256)
+            one = (a[at, cut].astype(F32) - bdot(left[0], right1[:, cut])).astype(BF16)
+            a[at, cut] = (one.astype(F32) - bdot(left[1], right2[:, cut])).astype(BF16)
+        store(block).start()
 
     def update(t):
         by_step(t, update_block)
@@ -463,7 +470,7 @@
     g_x.drain()
     g_y.drain()
     loop(1, 8, lambda d: y_copy(d).wait_send())
-    loop(0, ROWS // 256, lambda i: store(i).wait())
+    loop(0, ROWS // BLOCK, lambda i: store(i).wait())
 
 
 def scratch():
@@ -477,8 +484,9 @@
         vm((512, 128), F32), vm((512, 128), F32),
         vm((256, BLOCK), F32), vm((BLOCK, 256), BF16), vm((7, PIECE, 256), BF16),
         vm((2, NB, NB), F32),
-        vm((2, 2 * NB, 3 * NB), BF16), vm((2, 2 * NB, 2 * NB), BF16), vm((256, BLOCK), BF16), vm((256, BLOCK), BF16),
-        dma(()), dma((ROWS // 256,)), dma((7,)), dma((7,)),
+        vm((2 * NB, 3 * NB), BF16), vm((2, 2 * NB, 2 * NB), BF16), vm((256, BLOCK), BF16), vm((256, BLOCK), BF16),
+        vm((2, BLOCK, 256), BF16),
+        dma(()), dma((ROWS // BLOCK,)), dma((7,)), dma((7,)),
     ]
     for _ in range(2):
         shapes += [

time: 96.6 us -> 89.4 us (0.925)
  the two profiles are of different devices: /device:TPU:0 before, /device:TPU:6 now
where the time goes in v4:
time: 89.4 us; the launch traced here: 89.3 us
  Pallas kernels  86.2 us (96%)
  local copies, waits for them, and re-layouts  3.08 us (3%)
    pallas_call x1, Pallas kernels, per_device(): pl.pallas_call(kernel, out_shape=jax.ShapeDtypeStruct((ROWS, BLOCK), BF16...  86.2 us
    unnamed x3, local copies, waits for them, and re-layouts  3.08 us

profile of v4, /device:TPU:6, one launch (start us, length us, event | category | flops | bytes accessed | tf_op | source)
XLA Modules:
  0.0 89.3 jit_solution(15285757955354747450)
XLA Ops:
  0.0 0.0 copy-start
  0.0 0.9 copy-done
  0.9 86.2 %shard_map.28 = bf16[3072,768]{1,0:T(8,128)(2,1)S(1)} custom-call(bf16[3072,768]{1,0:T(8,128)(2,1)} %a_hbm.1, f32[2,96,128]{2,1,0:T(8,128)S(1)} %copy-done), custom_call_target="tpu_custom_call" | custom-call | flops 3700000000 | bytes 9437184 | tf_op jit(solution)/shard_map/pallas_call | solution.py:503
  87.1 2.2 %copy.4 = bf16[3072,768]{1,0:T(8,128)(2,1)} copy(bf16[3072,768]{1,0:T(8,128)(2,1)S(1)} %shard_map.28) | data formatting | bytes 9437184
Async XLA Ops:
  0.0 0.9 copy-start

commit v5 on v4

--- a/solution.py
+++ b/solution.py
@@ -36,6 +36,16 @@
         self.k = self.r % 2
         self.x = self.c // 8
         self.z = self.c % 8
+        self.target = 2 * self.x + self.z // 4
+        self.outside = self.r != self.target
+
+    def by_step(self, t, body):
+        for way in range(2 if 0 < t < 4 else 1):
+            src_z = (self.z - t + 8) % 8 if way == 0 else (self.z + t) % 8
+
+            @pl.when(src_z // 4 == self.k)
+            def _():
+                body(src_z % 4)
 
 
 def loop(lo, hi, body):
@@ -135,47 +145,100 @@
         self.piece = piece
         self.rows = rows
         self.cols = cols
-        self.cs, self.cq, self.xs, self.xq, self.zs, self.zq = sems
+        self.cs, self.cq, self.xs, self.xq, self.zs, self.zq, self.ts, self.tq, self.qs, self.qq, self.es, self.eq = sems
 
     def col_copy(self, d, owner):
         w = self.w
-        return rcopy(self.piece, self.cols.at[pl.ds(pl.multiple_of(owner * PIECE, PIECE), PIECE)],
+        return rcopy(self.piece, self.cols.at[:, pl.ds(pl.multiple_of(owner * PIECE, PIECE), PIECE)],
                      self.cs.at[d - 1], self.cq.at[d - 1], (w.r + d) % 8, w.c)
 
     def x_copy(self, d, owner):
         w = self.w
         at = pl.multiple_of((w.z % 4) * BLOCK + owner * PIECE, PIECE)
-        return rcopy(self.piece, self.rows.at[pl.ds(at, PIECE)], self.xs.at[d], self.xq.at[owner],
-                     2 * w.x + w.z // 4, ((w.x + d) % 4) * 8 + w.z)
+        return rcopy(self.piece.at[0], self.rows.at[0, pl.ds(at, PIECE)], self.xs.at[d], self.xq.at[owner],
+                     w.target, ((w.x + d) % 4) * 8 + w.z)
+
+    def turn_copy(self, owner):
+        w = self.w
+        at = pl.multiple_of((w.z % 4) * BLOCK + owner * PIECE, PIECE)
+        return rcopy(self.piece.at[1], self.rows.at[1, pl.ds(at, PIECE)], self.ts, self.tq.at[owner % 2],
+                     w.target, 8 * w.y + w.z)
+
+    def quarter_copy(self, way, t, at_z):
+        w = self.w
+        src_z = (at_z - t + 8) % 8 if way == 0 else (at_z + t) % 8
+        base = (src_z % 4) * BLOCK + w.x * 2 * PIECE
+        if t < 3:
+            part = self.rows.at[1, pl.ds(pl.multiple_of(base, 2 * PIECE), 2 * PIECE)]
+        else:
+            part = self.rows.at[1, pl.ds(pl.multiple_of(base + way * PIECE, PIECE), PIECE)]
+        to = (w.z + 1) % 8 if way == 0 else (w.z + 7) % 8
+        copy = rcopy(part, part, self.qs.at[way, t], self.qq.at[way, t], w.r, w.x * 8 + to)
+        return copy, src_z // 4 == w.k
+
+    def exchange_copy(self, d, block, owner_x):
+        w = self.w
+        at = pl.multiple_of(block * BLOCK + owner_x * 2 * PIECE, 2 * PIECE)
+        part = self.rows.at[1, pl.ds(at, 2 * PIECE)]
+        at = block * 3 + d - 1
+        return rcopy(part, part, self.es.at[at], self.eq.at[at], w.r, ((w.x + d) % 4) * 8 + w.z)
+
+    def quarter_step(self, t):
+        w = self.w
+        z = w.z
+        if t == 0:
+            @pl.when(z // 4 == w.k)
+            def _():
+                for kk in range(2):
+                    @pl.when(jnp.logical_not(jnp.logical_and(w.x == w.y, w.k == kk)))
+                    def _():
+                        self.turn_copy(2 * w.x + kk).wait_recv()
+        for way in range(2):
+            if t > 0:
+                copy, mine = self.quarter_copy(way, t - 1, (z + 7) % 8 if way == 0 else (z + 1) % 8)
+
+                @pl.when(mine)
+                def _():
+                    copy.wait_recv()
+            if t < 4:
+                copy, mine = self.quarter_copy(way, t, z)
+
+                @pl.when(mine)
+                def _():
+                    copy.start()
+        w.by_step(t, lambda block: loop(1, 4, lambda d: self.exchange_copy(d, block, w.x).start()))
+
+    def wait_exchange(self, t):
+        w = self.w
+        w.by_step(t, lambda block: loop(1, 4, lambda d: self.exchange_copy(d, block, (w.x - d + 4) % 4).wait_recv()))
 
     def z_copy(self, way, t, half, at_z):
         w = self.w
         src_z = (at_z - t + 8) % 8 if way == 0 else (at_z + t) % 8
         rows = BLOCK // 2
-        part = self.rows.at[pl.ds(pl.multiple_of((src_z % 4) * BLOCK + half * rows, rows), rows)]
+        part = self.rows.at[0, pl.ds(pl.multiple_of((src_z % 4) * BLOCK + half * rows, rows), rows)]
         to = (w.z + 1) % 8 if way == 0 else (w.z + 7) % 8
         copy = rcopy(part, part, self.zs.at[way, t, half], self.zq.at[way, t, half], w.r, w.x * 8 + to)
         return copy, src_z // 4 == w.k
 
     def start(self):
         w = self.w
-        for d in range(1, 4):
-            self.x_copy(d, w.r).start()
-        self_target = w.r == 2 * w.x + w.z // 4
-
-        @pl.when(jnp.logical_not(self_target))
+        loop(1, 4, lambda d: self.x_copy(d, w.r).start())
+
+        @pl.when(w.outside)
         def _():
             self.x_copy(0, w.r).start()
-
-        @pl.when(self_target)
+            self.turn_copy(w.r).start()
+
+        @pl.when(jnp.logical_not(w.outside))
         def _():
             at = pl.multiple_of((w.z % 4) * BLOCK + w.r * PIECE, PIECE)
-            self.rows[pl.ds(at, PIECE)] = self.piece[...]
+            self.rows[:, pl.ds(at, PIECE)] = self.piece[...]
 
     def start_cols(self):
         w = self.w
         loop(1, 8, lambda d: self.col_copy(d, w.r).start())
-        self.cols[pl.ds(pl.multiple_of(w.r * PIECE, PIECE), PIECE)] = self.piece[...]
+        self.cols[:, pl.ds(pl.multiple_of(w.r * PIECE, PIECE), PIECE)] = self.piece[...]
 
     def wait_x(self):
         w = self.w
@@ -210,6 +273,7 @@
                 @pl.when(mine)
                 def _():
                     copy.start()
+        self.quarter_step(t)
 
     def wait_cols(self):
         w = self.w
@@ -217,15 +281,24 @@
 
     def drain(self):
         w = self.w
-        for d in range(1, 4):
-            self.x_copy(d, w.r).wait_send()
-
-        @pl.when(w.r != 2 * w.x + w.z // 4)
+        loop(1, 4, lambda d: self.x_copy(d, w.r).wait_send())
+
+        @pl.when(w.outside)
         def _():
             self.x_copy(0, w.r).wait_send()
-
+            self.turn_copy(w.r).wait_send()
+
+        def sent(block):
+            loop(1, 4, lambda d: self.exchange_copy(d, block, w.x).wait_send())
+        loop(0, 4, sent)
         loop(1, 8, lambda d: self.col_copy(d, w.r).wait_send())
         for t in range(4):
+            for way in range(2):
+                copy, mine = self.quarter_copy(way, t, w.z)
+
+                @pl.when(mine)
+                def _():
+                    copy.wait_send()
             for way, half in self.halves(t):
                 copy, mine = self.z_copy(way, t, half, w.z)
 
@@ -269,13 +342,12 @@
     loop(1, 8, lambda d: greet((w.r + d) % 8, w.c))
     loop(1, 8, lambda d: greet(w.r, w.x * 8 + (w.z + d) % 8))
     loop(1, 4, lambda d: greet(w.r, (w.x + d) % 4 * 8 + w.z))
-    target = 2 * w.x + w.z // 4
-    loop(1, 4, lambda d: greet(target, (w.x + d) % 4 * 8 + w.z))
-    outside = w.r != target
-
-    @pl.when(outside)
+    loop(1, 4, lambda d: greet(w.target, (w.x + d) % 4 * 8 + w.z))
+
+    @pl.when(w.outside)
     def _():
-        greet(target, w.c)
+        greet(w.target, w.c)
+        greet(w.target, w.y * 8 + w.z)
 
     receives = w.z // 4 == w.k
 
@@ -287,7 +359,14 @@
                 greet(owner, 8 * w.y + w.z)
         loop(0, 8, one)
 
-    count = 20 + jnp.where(outside, 1, 0) + jnp.where(receives, jnp.where(w.x == w.y, 7, 8), 0)
+    @pl.when(receives)
+    def _():
+        for kk in range(2):
+            @pl.when(jnp.logical_not(jnp.logical_and(w.x == w.y, w.k == kk)))
+            def _():
+                greet(2 * w.x + kk, 8 * w.y + w.z)
+
+    count = 20 + jnp.where(w.outside, 2, 0) + jnp.where(receives, jnp.where(w.x == w.y, 8, 10), 0)
     pl.semaphore_wait(sem, count)
 
 
@@ -298,6 +377,10 @@
 
 def bdot(left, right, contract=((1,), (0,))):
     return lax.dot_general(left, right, (contract, ((), ())), preferred_element_type=F32)
+
+
+def pair(ref, at):
+    return jnp.concatenate([ref[0, at], ref[1, at]], axis=1)
 
 
 def kernel(a_hbm, pan, out, a, piece_x, piece_y, rows_x, rows_y, cols_x, cols_y,
@@ -307,15 +390,15 @@
     ar_g = AllReduce(w, gram, rest[:n_ar])
     ar_s = AllReduce(w, inner, rest[n_ar:2 * n_ar])
     sems = rest[2 * n_ar:]
-    g_x = Gather(w, piece_x, rows_x, cols_x, sems[0:6])
-    g_y = Gather(w, piece_y, rows_y, cols_y, sems[6:12])
+    g_x = Gather(w, piece_x, rows_x, cols_x, sems[0:12])
+    g_y = Gather(w, piece_y, rows_y, cols_y, sems[12:24])
 
     load = pltpu.make_async_copy(a_hbm, a, load_sem)
     load.start()
     v1 = pan[0]
     p2 = pan[1]
-    piece_x[:, 0:NB] = v1.astype(BF16)
-    piece_x[:, NB:] = p2.astype(BF16)
+    piece_x[0] = v1.astype(BF16)
+    piece_x[1] = p2.astype(BF16)
     barrier(w)
     g_x.start()
     both = jnp.concatenate([v1, p2], axis=1)
@@ -327,19 +410,12 @@
     def product_block(b):
         def tile(i):
             at = pl.ds(pl.multiple_of(b * BLOCK + i * 256, 256), 256)
-            yt[...] += bdot(rows_x[at], a[at], ((0,), (0,)))
+            yt[...] += bdot(pair(rows_x, at), a[at], ((0,), (0,)))
         loop(0, BLOCK // 256, tile)
 
-    def by_step(t, body):
-        for way in range(2 if 0 < t < 4 else 1):
-            src_z = (w.z - t + 8) % 8 if way == 0 else (w.z + t) % 8
-
-            @pl.when(src_z // 4 == w.k)
-            def _():
-                body(src_z % 4)
-
     def product(t):
-        by_step(t, product_block)
+        g_x.wait_exchange(t)
+        w.by_step(t, product_block)
 
     g_x.step(0)
     g_x.start_cols()
@@ -367,7 +443,8 @@
     loop(1, 8, lambda d: y_copy(d).start())
     g_x.wait_cols()
     hi, lo = split(yt[...])
-    s_t = bdot(hi, cols_x[...]) + bdot(lo, cols_x[...])
+    col_x = pair(cols_x, slice(0, BLOCK))
+    s_t = bdot(hi, col_x) + bdot(lo, col_x)
     inner[0:256] = s_t[:, 0:NB]
     inner[256:512] = s_t[:, NB:]
     ar_s.step1()
@@ -383,7 +460,8 @@
     total = y[pl.ds(pl.multiple_of(w.r * PIECE, PIECE), PIECE)].astype(F32)
     for d in range(7):
         total = total + y_in[d].astype(F32)
-    piece_y[...] = total.astype(BF16)
+    piece_y[0] = total[:, 0:NB].astype(BF16)
+    piece_y[1] = total[:, NB:].astype(BF16)
     g_y.start()
     ar_s.step2()
     invert(work, 5, 8)
@@ -427,8 +505,8 @@
     g_y.wait_cols()
 
     def form(x_ref, y_ref, at):
-        xt = x_ref[at]
-        yy = y_ref[at]
+        xt = pair(x_ref, at)
+        yy = pair(y_ref, at)
         both_x = bdot(xt, coef_x[...])
         wide = both_x[:, 0:2 * NB] + bdot(yy, coef_y[0]) + bdot(yy, coef_y[1])
         wb = wide.astype(BF16)
@@ -458,7 +536,8 @@
         store(block).start()
 
     def update(t):
-        by_step(t, update_block)
+        g_y.wait_exchange(t)
+        w.by_step(t, update_block)
 
     for t in range(4):
         update(t)
@@ -478,9 +557,9 @@
     dma = pltpu.SemaphoreType.DMA
     shapes = [
         vm((ROWS, BLOCK), BF16),
-        vm((PIECE, 256), BF16), vm((PIECE, 256), BF16),
-        vm((ROWS, 256), BF16), vm((ROWS, 256), BF16),
-        vm((BLOCK, 256), BF16), vm((BLOCK, 256), BF16),
+        vm((2, PIECE, NB), BF16), vm((2, PIECE, NB), BF16),
+        vm((2, ROWS, NB), BF16), vm((2, ROWS, NB), BF16),
+        vm((2, BLOCK, NB), BF16), vm((2, BLOCK, NB), BF16),
         vm((512, 128), F32), vm((512, 128), F32),
         vm((256, BLOCK), F32), vm((BLOCK, 256), BF16), vm((7, PIECE, 256), BF16),
         vm((2, NB, NB), F32),
@@ -495,7 +574,8 @@
             dma((7,)), dma((7,)), dma((3,)), dma((3,)), dma((7,)), dma((7,)), dma((3,)), dma((3,)), dma((7,)), dma((7,)),
         ]
     for _ in range(2):
-        shapes += [dma((7,)), dma((7,)), dma((4,)), dma((8,)), dma((2, 4, 2)), dma((2, 4, 2))]
+        shapes += [dma((7,)), dma((7,)), dma((4,)), dma((8,)), dma((2, 4, 2)), dma((2, 4, 2)),
+                   dma(()), dma((2,)), dma((2, 4)), dma((2, 4)), dma((12,)), dma((12,))]
     return shapes
 
 

time: 89.4 us -> 88.9 us (level)
  the two profiles are of different devices: /device:TPU:6 before, /device:TPU:1 now
where the time goes in v5:
time: 88.9 us; the launch traced here: 88.8 us
  Pallas kernels  85.7 us (96%)
  local copies, waits for them, and re-layouts  3.08 us (3%)
    pallas_call x1, Pallas kernels, per_device(): pl.pallas_call(kernel, out_shape=jax.ShapeDtypeStruct((ROWS, BLOCK), BF16...  85.7 us
    unnamed x3, local copies, waits for them, and re-layouts  3.08 us

profile of v5, /device:TPU:1, one launch (start us, length us, event | category | flops | bytes accessed | tf_op | source)
XLA Modules:
  0.0 88.8 jit_solution(8993186799968391634)
XLA Ops:
  0.0 0.0 copy-start
  0.0 0.9 %copy-done = f32[2,96,128]{2,1,0:T(8,128)S(1)} copy-done((f32[2,96,128]{2,1,0:T(8,128)S(1)}, f32[2,96,128]{2,1,0:T(8,128)}, u32[]{:S(2)}) %copy-start) | copy-done | bytes 98328
  0.9 85.7 %shard_map.28 = bf16[3072,768]{1,0:T(8,128)(2,1)S(1)} custom-call(bf16[3072,768]{1,0:T(8,128)(2,1)} %a_hbm.1, f32[2,96,128]{2,1,0:T(8,128)S(1)} %copy-done), custom_call_target="tpu_custom_call" | custom-call | flops 3700000000 | bytes 9437184 | tf_op jit(solution)/shard_map/pallas_call | solution.py:583
  86.6 2.2 %copy.4 = bf16[3072,768]{1,0:T(8,128)(2,1)} copy(bf16[3072,768]{1,0:T(8,128)(2,1)S(1)} %shard_map.28) | data formatting | bytes 9437184
Async XLA Ops:
  0.0 0.9 %copy-start = (f32[2,96,128]{2,1,0:T(8,128)S(1)}, f32[2,96,128]{2,1,0:T(8,128)}, u32[]{:S(2)}) copy-start(f32[2,96,128]{2,1,0:T(8,128)} %pan.1) | copy-start | bytes 294916
